TPU v7x, 768 devices: a whole 4x8x12 slice. The times are simulated.
768 devices in a mesh: gx: 8 (over y), gy: 8 (over x, core), gz: 12 (over z).
Axes of the slice: x: 4, y: 8, z: 12, core: 2. Of those that a mesh axis runs over, the one named last changes fastest.
Arguments:
- forcing: float32 [3, 24, 48, 2304], P(None, 'gx', 'gy', 'gz'), may hold values from -6 to 6
- initial_guess: float32 [3, 24, 48, 2304], P(None, 'gx', 'gy', 'gz'), may hold values from -4 to 4
- material: int32 [24, 48, 2304], P('gx', 'gy', 'gz'), may hold values from 0 to 3
- moduli: float32 [2, 4], replicated, may hold values from 0.5 to 4
- support: float32 [24, 48, 2304], P('gx', 'gy', 'gz'), may hold values from 0.05 to 0.5
- offsets: int32 [3], replicated, may hold values from 1 to 2, as said below
- aggregate_class: int32 [8, 16, 768], P('gx', 'gy', 'gz'), may hold values from 0 to 7
- class_blocks: float32 [8, 6, 6], replicated
Outputs:
- displacement: float32 [3, 24, 48, 2304], P(None, 'gx', 'gy', 'gz')
- coarse_correction: float32 [6, 8, 16, 768], P(None, 'gx', 'gy', 'gz')
Inputs may be any that keep to these rules, and one draw needn't show every extreme that they name: `offsets`: each entry is 1 or 2, and both values occur.
All inputs are finite; a program needn't handle non-finite values.
Results may differ from a plain program's by a relative error of at most 0.00029.
Values sent between devices are 32-bit elements; how exact they have to be, the bound alone decides.
No kernel may reach another device: no remote copies, remote signals or barrier semaphores. Data moves between devices by JAX's collectives and lax.ppermute only.
A program may use at most 32 MiB of HBM per device.

v0:
```python
import jax
import jax.numpy as jnp
from jax import lax
from jax.experimental import pallas as pl
from jax.experimental.pallas import tpu as pltpu
from jax.sharding import PartitionSpec as P

FINE_LOW = 0.25
FINE_HIGH = 2.5
COARSE_LOW = 0.2
COARSE_HIGH = 1.9

ROWS = 16
LANES = 256
ROW0 = 5
LANE0 = 16
EDGE = 16
SENT = slice(4, 12)
PLANES = 10
OWN_X, OWN_Y, OWN_Z = 3, 6, 192
FIELDS = 8
SIDE = 8
SPOTS = 7
COARSE_OWN = 64
COARSE_LANES = 70


def chebyshev(low, high, count):
    center = 0.5 * (high + low)
    spread = 0.5 * (high - low)
    ratio = center / spread
    weight = 1.0 / ratio
    steps = []
    for _ in range(1, count):
        following = 1.0 / (2.0 * ratio - weight)
        steps.append((following * weight, 2.0 * following / spread))
        weight = following
    return 1.0 / center, steps


FINE_FIRST, FINE_STEPS = chebyshev(FINE_LOW, FINE_HIGH, 2)
COARSE_FIRST, COARSE_STEPS = chebyshev(COARSE_LOW, COARSE_HIGH, 3)


def turned(value, shift, axis):
    shift = shift % value.shape[axis]
    return value if shift == 0 else pltpu.roll(value, shift, axis)


def following(value, axis):
    return turned(value, -1, axis)


def preceding(value, axis):
    return turned(value, 1, axis)


def plane_modes(value):
    ahead = following(value, 1)
    total, slope = value + ahead, ahead - value
    total_up, slope_up = following(total, 0), following(slope, 0)
    return {
        (0, 0): total + total_up,
        (1, 0): total_up - total,
        (0, 1): slope + slope_up,
        (1, 1): slope_up - slope,
    }


def element_modes(below, above, lame, shear):
    u = []
    for comp in range(3):
        modes = {}
        for key in ((0, 0), (1, 0), (0, 1), (1, 1)):
            first, second = below[comp][key], above[comp][key]
            if key != (0, 0):
                modes[(0,) + key] = first + second
            modes[(1,) + key] = second - first
        u.append(modes)
    x, y, z = u
    third = 1.0 / 3.0
    lame_b, shear_b = lame * third, shear * third
    shear_2 = shear + shear
    last = (lame + (shear_2 + shear_2)) * (1.0 / 9.0)
    f = [{}, {}, {}]
    divergence = lame * (x[1, 0, 0] + y[0, 1, 0] + z[0, 0, 1])
    f[0][1, 0, 0] = divergence + shear_2 * x[1, 0, 0]
    f[1][0, 1, 0] = divergence + shear_2 * y[0, 1, 0]
    f[2][0, 0, 1] = divergence + shear_2 * z[0, 0, 1]
    f[0][0, 1, 0] = f[1][1, 0, 0] = shear * (x[0, 1, 0] + y[1, 0, 0])
    f[0][0, 0, 1] = f[2][1, 0, 0] = shear * (x[0, 0, 1] + z[1, 0, 0])
    f[1][0, 0, 1] = f[2][0, 1, 0] = shear * (y[0, 0, 1] + z[0, 1, 0])
    for one, key_one, two, key_two in (
        (0, (1, 1, 0), 2, (0, 1, 1)),
        (0, (1, 0, 1), 1, (0, 1, 1)),
        (1, (1, 1, 0), 2, (1, 0, 1)),
    ):
        shared = lame_b * (u[one][key_one] + u[two][key_two])
        f[one][key_one] = shared + shear * u[one][key_one]
        f[two][key_two] = shared + shear * u[two][key_two]
    mixed = x[0, 1, 1] + y[1, 0, 1] + z[1, 1, 0]
    f[0][0, 1, 1] = shear_b * (mixed + x[0, 1, 1])
    f[1][1, 0, 1] = shear_b * (mixed + y[1, 0, 1])
    f[2][1, 1, 0] = shear_b * (mixed + z[1, 1, 0])
    for comp in range(3):
        f[comp][1, 1, 1] = last * u[comp][1, 1, 1]
    low, high = [], []
    for comp in range(3):
        down, up = {}, {}
        for key in ((0, 0), (1, 0), (0, 1), (1, 1)):
            slope = f[comp][(1,) + key]
            if key == (0, 0):
                down[key], up[key] = -slope, slope
            else:
                total = f[comp][(0,) + key]
                down[key], up[key] = total - slope, total + slope
        low.append(down)
        high.append(up)
    return low, high


def plane_forces(modes):
    parts = []
    for last in (0, 1):
        total, slope = modes[0, last], modes[1, last]
        parts.append((total - slope) + preceding(total + slope, 0))
    return (parts[0] - parts[1]) + preceding(parts[0] + parts[1], 1)


def stencil(read, elements, first, last, emit):
    below = [plane_modes(read(comp, first)) for comp in range(3)]
    carried = None
    for plane in range(first, last):
        above = [plane_modes(read(comp, plane + 1)) for comp in range(3)]
        low, high = element_modes(below, above, *elements(plane))
        if carried is not None:
            emit(
                plane,
                [
                    plane_forces({key: low[comp][key] + carried[comp][key] for key in low[comp]})
                    for comp in range(3)
                ],
            )
        below, carried = above, high


def picked_sums(values, weights):
    high = values.astype(jnp.bfloat16)
    left = values - high.astype(jnp.float32)
    middle = left.astype(jnp.bfloat16)
    low = (left - middle.astype(jnp.float32)).astype(jnp.bfloat16)
    weights = weights.astype(jnp.bfloat16)
    parts = [
        jnp.dot(part, weights, preferred_element_type=jnp.float32) for part in (low, middle, high)
    ]
    return (parts[0] + parts[1]) + parts[2]


def tile_row(plane, row, half):
    return ((plane * OWN_Y + row) * 2 + half) * FIELDS


def field_planes(guess, forcing, support, material, plane):
    for comp in range(3):
        yield comp, guess[comp, plane]
        yield 3 + comp, forcing[comp, plane]
    yield 6, support[plane]
    yield 7, material[plane].astype(jnp.float32)


def edges_kernel(
    guess_h, forcing_h, support_h, material_h, classes_h, low, high, guess, forcing, support, material,
    classes, done,
):
    pairs = (
        (guess_h, guess),
        (forcing_h, forcing),
        (support_h, support),
        (material_h, material),
        (classes_h, classes),
    )
    copies = [
        pltpu.make_async_copy(source, target, done.at[which])
        for which, (source, target) in enumerate(pairs)
    ]
    for copy in copies:
        copy.start()
    low[...] = jnp.zeros_like(low)
    high[...] = jnp.zeros_like(high)
    for copy in copies:
        copy.wait()
    kinds = classes[0].astype(jnp.float32)
    low[0, 0:2, 96:112] = kinds[:, 0:EDGE]
    high[0, 0:2, 96:112] = kinds[:, COARSE_OWN - EDGE :]
    for plane in range(OWN_X):
        for field, value in field_planes(guess, forcing, support, material, plane):
            for row in range(OWN_Y):
                line = value[row : row + 1]
                low[plane, field : field + 1, EDGE * row : EDGE * (row + 1)] = line[:, :EDGE]
                high[plane, field : field + 1, EDGE * row : EDGE * (row + 1)] = line[:, -EDGE:]


def pack_kernel(guess, forcing, support, material, classes, block, class_ext):
    first = 128 - LANE0
    block[...] = jnp.zeros_like(block)
    class_ext[...] = jnp.zeros_like(class_ext)
    class_ext[0:2, LANE0 : LANE0 + COARSE_OWN] = classes[0].astype(jnp.float32)
    for plane in range(OWN_X):
        for field, value in field_planes(guess, forcing, support, material, plane):
            for row in range(OWN_Y):
                line = value[row : row + 1]
                start = tile_row(plane, row, 0) + field
                block[start : start + 1, LANE0:128] = line[:, :first]
                start = tile_row(plane, row, 1) + field
                block[start : start + 1, 0 : OWN_Z - first] = line[:, first:]


def widen_kernel(block, low, high, class_ext, wide, class_wide, beyond):
    lane = lax.broadcasted_iota(jnp.int32, (8, 128), 1)
    end = LANE0 + OWN_Z - 128
    for plane in range(OWN_X):
        for row in range(OWN_Y):
            start = tile_row(plane, row, 0)
            wide[start : start + 8] = jnp.where(
                lane < LANE0, turned(low[plane], -EDGE * row, 1), block[start : start + 8]
            )
            start = tile_row(plane, row, 1)
            wide[start : start + 8] = jnp.where(
                (lane >= end) & (lane < end + EDGE),
                turned(high[plane], end - EDGE * row, 1),
                block[start : start + 8],
            )
    for row in range(OWN_Y):
        for half in range(2):
            start = tile_row(0, row, half)
            beyond[start : start + 8] = wide[start : start + 8]
            start = tile_row(1, row, half)
            beyond[start : start + 8] = turned(wide[start : start + 8], 3, 0)
    end = LANE0 + COARSE_OWN
    value = jnp.where(lane < LANE0, turned(low[0], -96, 1), class_ext[...])
    class_wide[...] = jnp.where(
        (lane >= end) & (lane < end + EDGE), turned(high[0], end - 96, 1), value
    )


def pre_kernel(
    moduli, scalars, planes, left, right, class_wide, chunk, remains, carry, smoothed, elements, nodes,
    fields, lame_s, shear_s, inverse_s, resid, step_one, step_two, sums_s,
):
    for plane in range(PLANES):
        for field in range(FIELDS):
            if plane == 0 and 3 <= field < 7 or plane == PLANES - 1 and field >= 3:
                continue
            at, held = (0, field + 3) if plane == PLANES - 1 else (plane, field)
            for half in range(2):
                lanes = slice(128 * half, 128 * half + 128)
                fields[field, plane, 0:1, lanes] = jnp.zeros((1, 128), jnp.float32)
                start = (at * 4 * 2 + half) * FIELDS + held
                fields[field, plane, 1:5, lanes] = left[pl.ds(start, 4, stride=16), :]
                start = (at * 5 * 2 + half) * FIELDS + held
                fields[field, plane, 11:16, lanes] = right[pl.ds(start, 5, stride=16), :]
                start = tile_row(at, 0, half) + held
                fields[field, plane, 5:11, lanes] = planes[pl.ds(start, 6, stride=16), :]
    table = [
        [moduli[which : which + 1, kind : kind + 1] for kind in range(4)]
        for which in range(2)
    ]
    carried = None
    for plane in range(PLANES - 1):
        kind = fields[7, plane]
        picked = []
        for which in range(2):
            value = jnp.where(kind < 2.5, table[which][2], table[which][3])
            value = jnp.where(kind < 1.5, table[which][1], value)
            picked.append(jnp.where(kind < 0.5, table[which][0], value))
        lame_s[plane] = picked[0]
        shear_s[plane] = picked[1]
        weight = (picked[0] + 4.0 * picked[1]) * (16.0 / 9.0)
        weight = weight + preceding(weight, 1)
        weight = weight + preceding(weight, 0)
        if carried is not None:
            inverse_s[plane] = 1.0 / (fields[6, plane] + weight + carried)
        carried = weight
    for plane in range(6):
        elements[0, plane] = lame_s[plane]
        elements[1, plane] = shear_s[plane]
    for plane in range(5):
        nodes[0, plane] = inverse_s[plane + 1]
        nodes[1, plane] = fields[6, plane + 1]

    shift_x, shift_y, shift_z = scalars[0, 0], scalars[0, 1], scalars[0, 2]
    base = shift_x - 1

    def coefficients(plane):
        return lame_s[base + plane], shear_s[base + plane]

    def first_step(plane, forces):
        at = base + plane
        support, inverse = fields[6, at], inverse_s[at]
        for comp in range(3):
            value = forces[comp] + support * fields[comp, at]
            value = fields[3 + comp, at] - value
            resid[comp, plane] = value
            step_one[comp, plane] = inverse * value * FINE_FIRST

    def second_step(plane, forces):
        at = base + plane
        support, inverse = fields[6, at], inverse_s[at]
        for comp in range(3):
            step = step_one[comp, plane]
            value = resid[comp, plane] - (forces[comp] + support * step)
            resid[comp, plane] = value
            update = FINE_STEPS[0][0] * step + FINE_STEPS[0][1] * (inverse * value)
            step_two[comp, plane] = update
            sums_s[plane - 2, comp] = fields[comp, at] + step + update

    def last_step(plane, forces):
        support = fields[6, base + plane]
        for comp in range(3):
            value = forces[comp] + support * step_two[comp, plane]
            value = resid[comp, plane] - value
            remains[plane - 3, comp] = value
            carry[plane - 3, comp] = value[SENT]

    stencil(lambda comp, plane: fields[comp, base + plane], coefficients, 0, 8, first_step)
    stencil(lambda comp, plane: step_one[comp, plane], coefficients, 1, 7, second_step)
    stencil(lambda comp, plane: step_two[comp, plane], coefficients, 2, 6, last_step)
    for comp in range(3):
        smoothed[0, comp] = sums_s[0, comp]
        smoothed[1, comp] = sums_s[2 - shift_x, comp]
        smoothed[2, comp] = sums_s[3 - shift_x, comp]
        carry[3, comp] = sums_s[4 - shift_x, comp][SENT]

    total = [remains[0, comp] + remains[1, comp] + remains[2, comp] for comp in range(3)]
    moment = [remains[2, comp] - remains[0, comp] for comp in range(3)]
    row = lax.broadcasted_iota(jnp.int32, (ROWS, LANES), 0)
    plain = jnp.zeros((ROWS, LANES), jnp.float32)
    lever = jnp.zeros((ROWS, LANES), jnp.float32)
    for half in range(2):
        place = row - (ROW0 + 3 * half) - shift_y
        inside = (place >= 0) & (place < 3)
        arm = (place - 1).astype(jnp.float32)

        def summed(value):
            return jnp.sum(jnp.where(inside, value, 0.0), axis=0, keepdims=True)

        sums = [summed(total[comp]) for comp in range(3)]
        lines = sums + [
            summed(arm * total[2]),
            summed(-moment[2]),
            summed(moment[1] - arm * total[0]),
        ]
        for comp in range(6):
            plain = jnp.where(row == 8 * half + comp, lines[comp], plain)
        lever = jnp.where(row == 8 * half + 3, -sums[1], lever)
        lever = jnp.where(row == 8 * half + 4, sums[0], lever)
    fine = lax.broadcasted_iota(jnp.int32, (LANES, 128), 0)
    coarse = lax.broadcasted_iota(jnp.int32, (LANES, 128), 1)
    place = fine - 3 * coarse + 2 * shift_z - 10
    inside = (place >= 0) & (place < 3) & (coarse < COARSE_LANES)
    sums_z = jnp.where(inside, 1.0, 0.0)
    arms_z = jnp.where(inside, (place - 1).astype(jnp.float32), 0.0)
    result = picked_sums(plain, sums_z) + picked_sums(lever, arms_z)
    kinds = pltpu.roll(class_wide[...], shift_z + (128 - 14), 1)
    line = lax.broadcasted_iota(jnp.int32, (8, 128), 0)
    lane = lax.broadcasted_iota(jnp.int32, (8, 128), 1)
    low = jnp.where(line == 6, kinds[0:1], result[0:8])
    high = jnp.where(line == 6, kinds[1:2], result[8:16])
    packed = jnp.where(lane < 64, turned(low, -3, 1), turned(high, 61, 1))
    ends = jnp.zeros((1, 128), jnp.float32)
    lane_one = lane[0:1]
    for half in range(2):
        for comp in range(7):
            base = 6 * comp + 3 * half
            source = turned((low, high)[half][comp : comp + 1], base, 1)
            first = (lane_one >= base) & (lane_one < base + 3)
            last = (lane_one >= base + 67) & (lane_one < base + 70)
            ends = jnp.where(first | last, source, ends)
    packed = jnp.where(line == 7, ends, packed)
    for target in range(SIDE * SIDE):
        chunk[target] = packed


def coarse_kernel(
    scalars, tables, received, rest, low, smoothed, elements, nodes, displacement, correction, right,
    matrix, step_a, step_b, error, spread_y, spread_z, work, step, resid, near,
):
    shift_x, shift_y, shift_z = scalars[0, 0], scalars[0, 1], scalars[0, 2]
    mine_x, mine_y = scalars[0, 3], scalars[0, 4]
    lane = lax.broadcasted_iota(jnp.int32, (8, 128), 1)
    line = lax.broadcasted_iota(jnp.int32, (8, 128), 0)
    even = line < 4
    middle = (lane >= 3) & (lane < 67)
    odd_shift = lax.rem(shift_y, 2)
    turn_even = lax.rem(SIDE + 2 - mine_y, SIDE)
    turn_odd = lax.rem(SIDE + 6 - mine_y - odd_shift, SIDE)
    for spot in range(SPOTS):
        at_x = lax.rem(mine_x - shift_x + (SIDE - 2 + spot), SIDE)
        ends = received[at_x, pl.ds(7, 8, stride=8), :]
        ends = [pltpu.roll(ends, turn_even, 0), pltpu.roll(ends, turn_odd, 0)]
        for comp in range(7):
            main = received[at_x, pl.ds(comp, 8, stride=8), :]
            main = [pltpu.roll(main, turn_even, 0), pltpu.roll(main, turn_odd, 0)]
            parts = []
            for which in range(2):
                half = odd_shift if which == 0 else 1 - odd_shift
                base = 6 * comp + 3 * half
                value = pltpu.roll(ends[which], lax.rem(128 - base, 128), 1)
                parts.append(jnp.where(middle, pltpu.roll(main[which], 3 + 64 * half, 1), value))
            value = jnp.where(even, parts[0], parts[1])
            right[comp, spot] = jnp.where(lane < COARSE_LANES, value, 0.0)

    kinds = [right[6, spot].astype(jnp.int32) for spot in range(SPOTS)]
    for entry in range(36):
        values = jnp.broadcast_to(tables[entry : entry + 1], (8, 128))
        for spot in range(SPOTS):
            matrix[entry, spot] = jnp.take_along_axis(
                values, kinds[spot], axis=1, mode="promise_in_bounds"
            )

    def product(values, spot):
        result = []
        for i in range(6):
            total = matrix[6 * i, spot] * values[0]
            for j in range(1, 6):
                total = total + matrix[6 * i + j, spot] * values[j]
            result.append(total)
        return result

    def neighbours(source, spot, comp):
        value = source[comp, spot]
        faces = source[comp, spot + 1] + source[comp, spot - 1]
        faces = faces + turned(value, 4, 0)
        faces = faces + jnp.where(even, turned(value, -3, 0), turned(value, 3, 0))
        return faces + turned(value, 1, 1) + turned(value, -1, 1)

    for spot in range(SPOTS):
        held = [right[comp, spot] for comp in range(6)]
        fresh = product(held, spot)
        for comp in range(6):
            step_a[comp, spot] = COARSE_FIRST * fresh[comp]
    scale_old, scale_new = COARSE_STEPS[0]
    for spot in range(1, SPOTS - 1):
        held = [right[comp, spot] for comp in range(6)]
        remains = []
        for comp in range(6):
            known = COARSE_FIRST * held[comp]
            value = held[comp] - (known - neighbours(step_a, spot, comp))
            remains.append(value)
            known = scale_old * known + scale_new * value
            right[comp, spot] = value - known
        fresh = product(remains, spot)
        for comp in range(6):
            step_b[comp, spot] = scale_old * step_a[comp, spot] + scale_new * fresh[comp]
    scale_old, scale_new = COARSE_STEPS[1]
    for spot in range(2, SPOTS - 2):
        remains = [right[comp, spot] + neighbours(step_b, spot, comp) for comp in range(6)]
        fresh = product(remains, spot)
        for comp in range(6):
            old = step_b[comp, spot]
            update = scale_old * old + scale_new * fresh[comp]
            error[comp, spot] = step_a[comp, spot] + old + update

    def window_row(inner):
        return 4 * lax.rem(inner, 2) + lax.div(inner, 2)

    for half in range(2):
        inner = window_row(half + shift_y + 2)
        for comp in range(6):
            value = error[comp, shift_x + 2, pl.ds(inner, 1), :]
            value = pltpu.roll(jnp.broadcast_to(value, (8, 128)), 126 - shift_z, 1)
            correction[comp, 0, half : half + 1, :] = value[0:1, :COARSE_OWN]

    row = lax.broadcasted_iota(jnp.int32, (ROWS, 128), 0)
    for near_x in range(3):
        for comp in range(6):
            plane = error[comp, near_x + 2]
            value = jnp.zeros((ROWS, 128), jnp.float32)
            for near_y in range(4):
                at = 4 * (near_y % 2) + near_y // 2 + 1
                inner = row - ROW0 - shift_y - 3 * (near_y - shift_y)
                value = jnp.where((inner >= 0) & (inner < 3), plane[at : at + 1], value)
            start = (comp * 3 + near_x) * ROWS
            spread_y[start : start + ROWS] = value
    coarse = lax.broadcasted_iota(jnp.int32, (128, LANES), 0)
    fine = lax.broadcasted_iota(jnp.int32, (128, LANES), 1)
    inner = fine - 3 * coarse + 2 * shift_z - 10
    copies = jnp.where((inner >= 0) & (inner < 3), 1.0, 0.0)
    wide = picked_sums(spread_y[...], copies)
    for which in range(18):
        spread_z[which] = wide[which * ROWS : (which + 1) * ROWS]

    row = lax.broadcasted_iota(jnp.int32, (ROWS, LANES), 0)
    fine = lax.broadcasted_iota(jnp.int32, (ROWS, LANES), 1)
    arm_y = (lax.rem(row + 4 - shift_y, 3) - 1).astype(jnp.float32)
    arm_z = (lax.rem(fine + 2 * shift_z + 2, 3) - 1).astype(jnp.float32)
    for plane in range(7):
        ahead = plane - 2 - shift_x + 6
        near_x = lax.div(ahead, 3) - 2 + shift_x
        arm_x = (lax.rem(ahead, 3) - 1).astype(jnp.float32)
        e = [spread_z[comp * 3 + near_x] for comp in range(6)]
        work[0, plane] = e[0] + e[4] * arm_z - e[5] * arm_y
        work[1, plane] = e[1] + e[5] * arm_x - e[3] * arm_z
        work[2, plane] = e[2] + e[3] * arm_y - e[4] * arm_x

    near[...] = jnp.zeros_like(near)
    near[:, :, SENT] = low[...]
    one = (shift_x == 1).astype(jnp.float32)
    two = 1.0 - one

    def remaining(at, comp):
        if at < 2:
            return near[at + 2 - shift_x, comp]
        if at == 2:
            return one * rest[0, comp] + two * near[2, comp]
        return rest[at - 1 - shift_x, comp]

    def first_step(plane, forces):
        at = plane - 1
        for comp in range(3):
            value = forces[comp] + nodes[1, at] * work[comp, plane]
            value = remaining(at, comp) - value
            resid[comp, at] = value
            step[comp, at] = nodes[0, at] * value * FINE_FIRST

    def last_step(plane, forces):
        for comp in range(3):
            old = step[comp, plane]
            value = resid[comp, plane] - (forces[comp] + nodes[1, plane] * old)
            update = FINE_STEPS[0][0] * old + FINE_STEPS[0][1] * (nodes[0, plane] * value)
            start = smoothed[plane - 1, comp]
            if plane == 1:
                start = one * start + two * near[3, comp]
            value = start + work[comp, plane + 1] + old + update
            displacement[comp, plane - 1] = value[
                ROW0 : ROW0 + OWN_Y, LANE0 : LANE0 + OWN_Z
            ]

    stencil(
        lambda comp, plane: work[comp, plane],
        lambda plane: (elements[0, plane], elements[1, plane]),
        0,
        6,
        first_step,
    )
    stencil(
        lambda comp, plane: step[comp, plane],
        lambda plane: (elements[0, plane + 1], elements[1, plane + 1]),
        0,
        4,
        last_step,
    )


def tables_kernel(blocks, tables):
    rows = []
    for i in range(6):
        row = [blocks[6 * i + j : 6 * i + j + 1] for j in range(6)]
        row[i] = row[i] + 6.0
        one = jnp.ones_like(row[0])
        rows.append(row + [one if i == j else jnp.zeros_like(one) for j in range(6)])
    for pivot in range(6):
        scaled = [value / rows[pivot][pivot] for value in rows[pivot]]
        for i in range(6):
            factor = rows[i][pivot]
            if i != pivot:
                rows[i] = [value - factor * line for value, line in zip(rows[i], scaled)]
        rows[pivot] = scaled
    tables[36:40] = jnp.zeros_like(tables[36:40])
    for i in range(6):
        for j in range(6):
            entry = 6 * i + j
            tables[entry : entry + 1] = rows[i][6 + j]


def passed_along(value, axis, steps):
    count = lax.axis_size(axis)
    pairs = [(source, (source + steps) % count) for source in range(count)]
    return lax.ppermute(value, axis, pairs)


VMEM = pl.BlockSpec(memory_space=pltpu.VMEM)
EDGES_VMEM = 64 * 1024 * 1024 - 512 * 1024


def call(kernel, arrays, shapes, scratch=(), work=1_000_000):
    return pl.pallas_call(
        kernel,
        out_shape=[jax.ShapeDtypeStruct(shape, jnp.float32) for shape in shapes],
        in_specs=[VMEM] * len(arrays),
        out_specs=[VMEM] * len(shapes),
        scratch_shapes=[pltpu.VMEM(shape, jnp.float32) for shape in scratch],
        compiler_params=pltpu.CompilerParams(vmem_limit_bytes=48 * 1024 * 1024),
        cost_estimate=pl.CostEstimate(flops=work, bytes_accessed=work, transcendentals=0),
    )(*arrays)


def pack_edges(*arrays):
    return pl.pallas_call(
        edges_kernel,
        out_shape=[jax.ShapeDtypeStruct((OWN_X, FIELDS, 128), jnp.float32)] * 2,
        in_specs=[pl.BlockSpec(memory_space=pltpu.HBM)] * len(arrays),
        out_specs=[VMEM] * 2,
        scratch_shapes=[pltpu.VMEM(array.shape, array.dtype) for array in arrays]
        + [pltpu.SemaphoreType.DMA((len(arrays),))],
        compiler_params=pltpu.CompilerParams(vmem_limit_bytes=EDGES_VMEM),
    )(*arrays)


def pack(*arrays):
    shapes = [(OWN_X * OWN_Y * 2 * FIELDS, 128), (8, 128)]
    return call(pack_kernel, arrays, shapes, work=20_000_000)


def widen(block, low, high, class_ext):
    shapes = [(OWN_X * OWN_Y * 2 * FIELDS, 128), (8, 128), (2 * OWN_Y * 2 * FIELDS, 128)]
    return call(widen_kernel, (block, low, high, class_ext), shapes)


def pre_smooth(moduli, scalars, planes, left, right, class_wide):
    plane = (ROWS, LANES)
    return call(
        pre_kernel,
        (moduli, scalars, planes, left, right, class_wide),
        [(SIDE * SIDE, 8, 128), (3, 3) + plane, (4, 3, 8, LANES), (3, 3) + plane]
        + [(2, 6) + plane, (2, 5) + plane],
        [(FIELDS, PLANES) + plane] + [(PLANES,) + plane] * 3
        + [(3, 9) + plane, (3, 9) + plane, (3, 9) + plane, (5, 3) + plane],
    )


def coarse_and_post(scalars, tables, received, rest, low, smoothed, elements, nodes):
    plane = (ROWS, LANES)
    spots = (SPOTS, 8, 128)
    return call(
        coarse_kernel,
        (scalars, tables, received, rest, low, smoothed, elements, nodes),
        [(3, OWN_X, OWN_Y, OWN_Z), (6, 1, 2, COARSE_OWN)],
        [(7,) + spots, (36,) + spots, (6,) + spots, (6,) + spots, (6,) + spots]
        + [(18 * ROWS, 128), (18,) + plane, (3, 7) + plane, (3, 5) + plane, (3, 5) + plane]
        + [(4, 3) + plane],
    )


def coarse_tables(class_blocks):
    entries = jnp.transpose(class_blocks.reshape(8, 36))
    entries = jnp.pad(entries, ((0, 4), (0, 120)))
    return call(tables_kernel, (entries,), [(40, 128)])[0]


def body(forcing, initial_guess, material, moduli, support, offsets, aggregate_class, class_blocks):
    tables = coarse_tables(class_blocks)
    place = jnp.stack([lax.axis_index("gx"), lax.axis_index("gy")]).astype(jnp.int32)
    scalars = jnp.concatenate([offsets, place]).reshape(1, 5)
    arrays = (initial_guess, forcing, support, material, aggregate_class)
    low, high = pack_edges(*arrays)
    from_low = passed_along(high, "gz", 1)
    from_high = passed_along(low, "gz", -1)
    block, class_ext = pack(*arrays)
    own, class_wide, beyond = widen(block, from_low, from_high, class_ext)
    own = own.reshape(OWN_X, OWN_Y, 2 * FIELDS, 128)
    before = passed_along(own[1:], "gx", 1)
    after = passed_along(own, "gx", -1)
    beyond = passed_along(beyond.reshape(2, OWN_Y, 2 * FIELDS, 128), "gx", -2)
    before, after = lax.optimization_barrier((before, after))
    field = lax.broadcasted_iota(jnp.int32, (OWN_Y, 2 * FIELDS, 128), 1) % FIELDS
    beyond = jnp.where(((field >= 3) & (field < 6))[None] | (jnp.arange(2) == 0)[:, None, None, None], beyond, 0.0)
    beyond = lax.optimization_barrier(beyond)
    mixed = jnp.where((field >= 3) & (field < 6), beyond[1], before[0])
    planes = jnp.concatenate([mixed[None], before[1:], own, after, beyond[:1]], axis=0)
    left = passed_along(planes[:, 2:], "gy", 1).reshape(-1, 128)
    right = passed_along(planes[:, :5], "gy", -1).reshape(-1, 128)
    chunk, rest, carry, smoothed, elements, nodes = pre_smooth(
        moduli * (1.0 / 16.0), scalars, planes.reshape(-1, 128), left, right, class_wide
    )
    received = lax.all_to_all(chunk, ("gx", "gy"), 0, 0, tiled=True)
    received = received.reshape(SIDE, SIDE * 8, 128)
    from_before = passed_along(carry, "gx", 1)
    displacement, correction = coarse_and_post(
        scalars, tables, received, rest, from_before, smoothed, elements, nodes
    )
    return displacement, correction


def solution(mesh):
    placed = (
        P(None, "gx", "gy", "gz"),
        P(None, "gx", "gy", "gz"),
        P("gx", "gy", "gz"),
        P(),
        P("gx", "gy", "gz"),
        P(),
        P("gx", "gy", "gz"),
        P(),
    )
    return jax.shard_map(
        body,
        mesh=mesh,
        in_specs=placed,
        out_specs=(P(None, "gx", "gy", "gz"), P(None, "gx", "gy", "gz")),
        check_vma=False,
    )
```

profile of v0, /device:TPU:1, one launch (start us, length us, event | category | flops | bytes accessed | tf_op | source)
XLA Modules:
  0.0 72.0 jit_solution(7874300604862819645)
XLA Ops:
  0.6 0.0 copy-start.1
  0.6 0.0 copy-start
  0.7 0.0 copy-start.3
  0.7 0.0 copy-start.4
  0.7 2.0 %shard_map.97 = (f32[3,8,128]{2,1,0:T(8,128)}, f32[3,8,128]{2,1,0:T(8,128)}) custom-call(f32[3,3,6,192]{3,2,1,0:T(8,128)} %guess_h.1, f32[3,3,6,192]{3,2,1,0:T(8,128)} %forcing_h.1, f32[3,6,192]{2,1,0:T(8,128)} %support_h.1, s32[3,6,192]{2,1,0:T(8,128)} %material_h.1, s32[1,2,64]{2,1,0:T(2,128)} %classes_h.1), custom_call_target="tpu_custom_call" | custom-call | tf_op jit(solution)/shard_map/pallas_call | solution.py:599
  2.6 0.0 copy-start.2
  2.6 4.8 %collective-permute-start = (f32[3,8,128]{2,1,0:T(8,128)}, f32[3,8,128]{2,1,0:T(8,128)S(1)}, u32[]{:S(2)}, u32[]{:S(2)}) collective-permute-start(f32[3,8,128]{2,1,0:T(8,128)} %get-tuple-element.18), channel_id=1, source_target_pairs={{0,1},{1,2},{2,3},{3,4},{4,5},{5,6},{6,7},{7,8},{8,9},{9,10},{10,1... | collective-permute-start | bytes 36872 | tf_op jit(solution)/shard_map/ppermute | solution.py:579
  7.5 12.2 %collective-permute-start.1 = (f32[3,8,128]{2,1,0:T(8,128)}, f32[3,8,128]{2,1,0:T(8,128)S(1)}, u32[]{:S(2)}, u32[]{:S(2)}) collective-permute-start(f32[3,8,128]{2,1,0:T(8,128)} %get-tuple-element.19), channel_id=1, source_target_pairs={{0,11},{1,0},{2,1},{3,2},{4,3},{5,4},{6,5},{7,6},{8,7},{9,8},{10,9... | collective-permute-start | bytes 36872 | tf_op jit(solution)/shard_map/ppermute | solution.py:579
  19.7 0.1 fusion.2
  19.8 0.0 copy-done.1
  19.8 0.0 copy-done
  19.8 0.0 copy-done.3
  19.8 0.0 copy-done.4
  19.9 0.0 copy-done.2
  19.9 0.1 shard_map.96
  20.0 0.0 collective-permute-done.low
  20.0 0.7 collective-permute-done.1.high
  20.7 0.1 shard_map.98
  20.8 5.9 %collective-permute-start.2 = (f32[2,6,16,128]{3,2,1,0:T(8,128)S(1)}, f32[2,6,16,128]{3,2,1,0:T(8,128)S(1)}, u32[]{:S(2)}, u32[]{:S(2)}) collective-permute-start(f32[2,6,16,128]{3,2,1,0:T(8,128)S(1)} %bitcast.20), channel_id=1, source_target_pairs={{0,576},{96,672},{192,0},{288,96},{384,192},{480,288},{576,384},{6... | collective-permute-start | bytes 294920 | tf_op jit(solution)/shard_map/ppermute | solution.py:579
  26.8 3.0 %collective-permute-start.4 = (f32[3,6,16,128]{3,2,1,0:T(8,128)S(1)}, f32[3,6,16,128]{3,2,1,0:T(8,128)S(1)}, u32[]{:S(2)}, u32[]{:S(2)}) collective-permute-start(f32[3,6,16,128]{3,2,1,0:T(8,128)S(1)} %bitcast.16), channel_id=1, source_target_pairs={{0,672},{96,0},{192,96},{288,192},{384,288},{480,384},{576,480},{6... | collective-permute-start | bytes 442376 | tf_op jit(solution)/shard_map/ppermute | solution.py:579
  29.7 2.3 %collective-permute-start.3 = (f32[2,6,16,128]{3,2,1,0:T(8,128)S(1)}, f32[2,6,16,128]{3,2,1,0:T(8,128)S(1)}, u32[]{:S(2)}, u32[]{:S(2)}) collective-permute-start(f32[2,6,16,128]{3,2,1,0:T(8,128)S(1)} %bitcast.21), channel_id=1, source_target_pairs={{0,96},{96,192},{192,288},{288,384},{384,480},{480,576},{576,672},... | collective-permute-start | bytes 294920 | tf_op jit(solution)/shard_map/ppermute | solution.py:579
  32.1 0.0 collective-permute-done.2
  32.1 0.1 or_select_fusion
  32.1 4.2 %collective-permute-done.3 = f32[2,6,16,128]{3,2,1,0:T(8,128)S(1)} collective-permute-done((f32[2,6,16,128]{3,2,1,0:T(8,128)S(1)}, f32[2,6,16,128]{3,2,1,0:T(8,128)S(1)}, u32[]{:S(2)}, u32[]{:S(2)}) %collective-permute-start.3) | collective-permute-done | bytes 98336 | tf_op jit(solution)/shard_map/ppermute | solution.py:579
  36.3 0.0 collective-permute-done.4
  36.3 0.1 fusion
  36.5 3.2 %collective-permute-start.6 = (f32[9,5,16,128]{3,2,1,0:T(8,128)S(1)}, f32[9,5,16,128]{3,2,1,0:T(8,128)S(1)}, u32[]{:S(2)}, u32[]{:S(2)}) collective-permute-start(f32[9,5,16,128]{3,2,1,0:T(8,128)S(1)} %slice.35), channel_id=1, source_target_pairs={{0,84},{12,0},{24,12},{36,24},{48,36},{60,48},{72,60},{84,72},{1,8... | collective-permute-start | bytes 1105928 | tf_op jit(solution)/shard_map/ppermute | solution.py:579
  39.8 1.1 %collective-permute-start.5 = (f32[9,4,16,128]{3,2,1,0:T(8,128)S(1)}, f32[9,4,16,128]{3,2,1,0:T(8,128)S(1)}, u32[]{:S(2)}, u32[]{:S(2)}) collective-permute-start(f32[9,4,16,128]{3,2,1,0:T(8,128)S(1)} %slice.34), channel_id=1, source_target_pairs={{0,12},{12,24},{24,36},{36,48},{48,60},{60,72},{72,84},{84,0},{1,1... | collective-permute-start | bytes 884744 | tf_op jit(solution)/shard_map/ppermute | solution.py:579
  40.9 0.0 copy-start.7
  40.9 0.7 copy-done.7
  41.6 0.0 copy-start.6
  41.6 0.1 add_bitcast_fusion.scalars
  41.6 0.6 copy-done.6
  42.2 2.3 %collective-permute-done.5 = f32[9,4,16,128]{3,2,1,0:T(8,128)S(1)} collective-permute-done((f32[9,4,16,128]{3,2,1,0:T(8,128)S(1)}, f32[9,4,16,128]{3,2,1,0:T(8,128)S(1)}, u32[]{:S(2)}, u32[]{:S(2)}) %collective-permute-start.5) | collective-permute-done | bytes 294944 | tf_op jit(solution)/shard_map/ppermute | solution.py:579
  44.6 1.8 %collective-permute-done.6 = f32[9,5,16,128]{3,2,1,0:T(8,128)S(1)} collective-permute-done((f32[9,5,16,128]{3,2,1,0:T(8,128)S(1)}, f32[9,5,16,128]{3,2,1,0:T(8,128)S(1)}, u32[]{:S(2)}, u32[]{:S(2)}) %collective-permute-start.6) | collective-permute-done | bytes 368672 | tf_op jit(solution)/shard_map/ppermute | solution.py:579
  46.3 3.8 %shard_map.99 = (f32[64,8,128]{2,1,0:T(8,128)}, f32[3,3,16,256]{3,2,1,0:T(8,128)S(1)}, f32[4,3,8,256]{3,2,1,0:T(8,128)S(1)}, f32[3,3,16,256]{3,2,1,0:T(8,128)S(1...) custom-call(f32[2,4]{1,0:T(2,128)S(1)} %broadcast_multiply_fusion.moduli, ...), custom_call_target="tpu_custom_call" | custom-call | flops 1000000 | bytes 1000000 | tf_op jit(solution)/shard_map/pallas_call | solution.py:587
  50.2 0.0 copy-start.5
  50.2 5.1 %all-to-all-start = ((f32[64,8,128]{2,1,0:T(8,128)}), f32[64,8,128]{2,1,0:T(8,128)S(1)}, u32[]{:S(2)}, u32[]{:S(2)}) async-start(f32[64,8,128]{2,1,0:T(8,128)} %get-tuple-element.26), calls=%async_computation | async-start | bytes 524288 | tf_op jit(solution)/shard_map/all_to_all | solution.py:676
  55.2 3.3 %collective-permute-start.7 = (f32[4,3,8,256]{3,2,1,0:T(8,128)S(1)}, f32[4,3,8,256]{3,2,1,0:T(8,128)S(1)}, u32[]{:S(2)}, u32[]{:S(2)}) collective-permute-start(f32[4,3,8,256]{3,2,1,0:T(8,128)S(1)} %get-tuple-element.28), channel_id=1, source_target_pairs={{0,96},{96,192},{192,288},{288,384},{384,480},{480,576},{576,672},... | collective-permute-start | bytes 294920 | tf_op jit(solution)/shard_map/ppermute | solution.py:579
  58.5 0.0 copy-done.5
  58.6 0.1 copy.13
  58.7 0.1 shard_map.95.tables
  58.8 7.6 %collective-permute-done.7.low = f32[4,3,8,256]{3,2,1,0:T(8,128)S(1)} collective-permute-done((f32[4,3,8,256]{3,2,1,0:T(8,128)S(1)}, f32[4,3,8,256]{3,2,1,0:T(8,128)S(1)}, u32[]{:S(2)}, u32[]{:S(2)}) %collective-permute-start.7) | collective-permute-done | bytes 98336 | tf_op jit(solution)/shard_map/ppermute | solution.py:579
  66.4 2.0 %all-to-all-done = f32[64,8,128]{2,1,0:T(8,128)S(1)} async-done(((f32[64,8,128]{2,1,0:T(8,128)}), f32[64,8,128]{2,1,0:T(8,128)S(1)}, u32[]{:S(2)}, u32[]{:S(2)}) %all-to-all-start) | async-done | bytes 262176 | tf_op jit(solution)/shard_map/all_to_all | solution.py:676
  68.5 3.5 %shard_map.100 = (f32[3,3,6,192]{3,2,1,0:T(8,128)}, f32[6,1,2,64]{3,2,1,0:T(2,128)}) custom-call(s32[1,5]{1,0:T(1,128)S(1)} %add_bitcast_fusion.scalars, f32[40,128]{1,0:T(8,128)S(1)} %shard_map.95.tables, f32[8,64,128]{2,1,0:T(8,128)S(1)} %bitcast.15, f32[3,3,16,256]{3,2,1,0:T(8,128)S(1)} %get-tuple-element.27.rest, ...), custom_call_target="tpu_custom_call" | custom-call | flops 1000000 | bytes 1000000 | tf_op jit(solution)/shard_map/pallas_call | solution.py:587
  (13 shorter events, 0.1 us)
Async XLA Ops:
  0.6 19.2 %copy-start.1 = (f32[3,3,6,192]{3,2,1,0:T(8,128)S(1)}, f32[3,3,6,192]{3,2,1,0:T(8,128)}, u32[]{:S(2)}) copy-start(f32[3,3,6,192]{3,2,1,0:T(8,128)} %forcing_h.1) | copy-start | bytes 124420
  0.6 19.2 %copy-start = (f32[3,3,6,192]{3,2,1,0:T(8,128)S(1)}, f32[3,3,6,192]{3,2,1,0:T(8,128)}, u32[]{:S(2)}) copy-start(f32[3,3,6,192]{3,2,1,0:T(8,128)} %guess_h.1) | copy-start | bytes 124420
  0.7 19.2 %copy-start.3 = (s32[3,6,192]{2,1,0:T(8,128)S(1)}, s32[3,6,192]{2,1,0:T(8,128)}, u32[]{:S(2)}) copy-start(s32[3,6,192]{2,1,0:T(8,128)} %material_h.1) | copy-start | bytes 41476
  0.7 19.2 %copy-start.4 = (s32[1,2,64]{2,1,0:T(2,128)S(1)}, s32[1,2,64]{2,1,0:T(2,128)}, u32[]{:S(2)}) copy-start(s32[1,2,64]{2,1,0:T(2,128)} %classes_h.1) | copy-start | bytes 1540
  2.6 17.2 %copy-start.2 = (f32[3,6,192]{2,1,0:T(8,128)S(1)}, f32[3,6,192]{2,1,0:T(8,128)}, u32[]{:S(2)}) copy-start(f32[3,6,192]{2,1,0:T(8,128)} %support_h.1) | copy-start | bytes 41476
  2.6 17.4 %collective-permute-start = (f32[3,8,128]{2,1,0:T(8,128)}, f32[3,8,128]{2,1,0:T(8,128)S(1)}, u32[]{:S(2)}, u32[]{:S(2)}) collective-permute-start(f32[3,8,128]{2,1,0:T(8,128)} %get-tuple-element.18), channel_id=1, source_target_pairs={{0,1},{1,2},{2,3},{3,4},{4,5},{5,6},{6,7},{7,8},{8,9},{9,10},{10,1... | collective-permute-start | bytes 36872 | tf_op jit(solution)/shard_map/ppermute | solution.py:579
  7.5 13.3 %collective-permute-start.1 = (f32[3,8,128]{2,1,0:T(8,128)}, f32[3,8,128]{2,1,0:T(8,128)S(1)}, u32[]{:S(2)}, u32[]{:S(2)}) collective-permute-start(f32[3,8,128]{2,1,0:T(8,128)} %get-tuple-element.19), channel_id=1, source_target_pairs={{0,11},{1,0},{2,1},{3,2},{4,3},{5,4},{6,5},{7,6},{8,7},{9,8},{10,9... | collective-permute-start | bytes 36872 | tf_op jit(solution)/shard_map/ppermute | solution.py:579
  20.8 11.2 %collective-permute-start.2 = (f32[2,6,16,128]{3,2,1,0:T(8,128)S(1)}, f32[2,6,16,128]{3,2,1,0:T(8,128)S(1)}, u32[]{:S(2)}, u32[]{:S(2)}) collective-permute-start(f32[2,6,16,128]{3,2,1,0:T(8,128)S(1)} %bitcast.20), channel_id=1, source_target_pairs={{0,576},{96,672},{192,0},{288,96},{384,192},{480,288},{576,384},{6... | collective-permute-start | bytes 294920 | tf_op jit(solution)/shard_map/ppermute | solution.py:579
  26.8 9.6 %collective-permute-start.4 = (f32[3,6,16,128]{3,2,1,0:T(8,128)S(1)}, f32[3,6,16,128]{3,2,1,0:T(8,128)S(1)}, u32[]{:S(2)}, u32[]{:S(2)}) collective-permute-start(f32[3,6,16,128]{3,2,1,0:T(8,128)S(1)} %bitcast.16), channel_id=1, source_target_pairs={{0,672},{96,0},{192,96},{288,192},{384,288},{480,384},{576,480},{6... | collective-permute-start | bytes 442376 | tf_op jit(solution)/shard_map/ppermute | solution.py:579
  29.7 6.6 %collective-permute-start.3 = (f32[2,6,16,128]{3,2,1,0:T(8,128)S(1)}, f32[2,6,16,128]{3,2,1,0:T(8,128)S(1)}, u32[]{:S(2)}, u32[]{:S(2)}) collective-permute-start(f32[2,6,16,128]{3,2,1,0:T(8,128)S(1)} %bitcast.21), channel_id=1, source_target_pairs={{0,96},{96,192},{192,288},{288,384},{384,480},{480,576},{576,672},... | collective-permute-start | bytes 294920 | tf_op jit(solution)/shard_map/ppermute | solution.py:579
  36.5 9.8 %collective-permute-start.6 = (f32[9,5,16,128]{3,2,1,0:T(8,128)S(1)}, f32[9,5,16,128]{3,2,1,0:T(8,128)S(1)}, u32[]{:S(2)}, u32[]{:S(2)}) collective-permute-start(f32[9,5,16,128]{3,2,1,0:T(8,128)S(1)} %slice.35), channel_id=1, source_target_pairs={{0,84},{12,0},{24,12},{36,24},{48,36},{60,48},{72,60},{84,72},{1,8... | collective-permute-start | bytes 1105928 | tf_op jit(solution)/shard_map/ppermute | solution.py:579
  39.8 4.8 %collective-permute-start.5 = (f32[9,4,16,128]{3,2,1,0:T(8,128)S(1)}, f32[9,4,16,128]{3,2,1,0:T(8,128)S(1)}, u32[]{:S(2)}, u32[]{:S(2)}) collective-permute-start(f32[9,4,16,128]{3,2,1,0:T(8,128)S(1)} %slice.34), channel_id=1, source_target_pairs={{0,12},{12,24},{24,36},{36,48},{48,60},{60,72},{72,84},{84,0},{1,1... | collective-permute-start | bytes 884744 | tf_op jit(solution)/shard_map/ppermute | solution.py:579
  40.9 0.7 copy-start.7
  41.6 0.7 copy-start.6
  50.2 8.4 %copy-start.5 = (f32[8,6,6]{2,0,1:T(8,128)S(1)}, f32[8,6,6]{2,0,1:T(8,128)}, u32[]{:S(2)}) copy-start(f32[8,6,6]{2,0,1:T(8,128)} %param.15) | copy-start | bytes 3460
  50.2 18.3 %all-to-all-start = ((f32[64,8,128]{2,1,0:T(8,128)}), f32[64,8,128]{2,1,0:T(8,128)S(1)}, u32[]{:S(2)}, u32[]{:S(2)}) async-start(f32[64,8,128]{2,1,0:T(8,128)} %get-tuple-element.26), calls=%async_computation | async-start | bytes 524288 | tf_op jit(solution)/shard_map/all_to_all | solution.py:676
  55.2 11.2 %collective-permute-start.7 = (f32[4,3,8,256]{3,2,1,0:T(8,128)S(1)}, f32[4,3,8,256]{3,2,1,0:T(8,128)S(1)}, u32[]{:S(2)}, u32[]{:S(2)}) collective-permute-start(f32[4,3,8,256]{3,2,1,0:T(8,128)S(1)} %get-tuple-element.28), channel_id=1, source_target_pairs={{0,96},{96,192},{192,288},{288,384},{384,480},{480,576},{576,672},... | collective-permute-start | bytes 294920 | tf_op jit(solution)/shard_map/ppermute | solution.py:579
where the time goes:
time: 72.5 us; the launch traced here: 72 us
  starting transfers between devices  41 us (57%)
  waiting for transfers between devices  18.7 us (26%)
  Pallas kernels  9.62 us (13%)
  local copies, waits for them, and re-layouts  1.5 us (2%)
  between operations  0.9 us (1%)
    ppermute x8, starting transfers between devices, passed_along(): return lax.ppermute(value, axis, pairs)  35.9 us
    ppermute x8, waiting for transfers between devices, passed_along(): return lax.ppermute(value, axis, pairs)  16.6 us
    pallas_call x5, Pallas kernels, call(): pl.pallas_call(kernel, out_shape=[jax.ShapeDtypeStruct(shape, jnp.float32...  7.67 us
    all_to_all x1, starting transfers between devices, body(): received = lax.all_to_all(chunk, ('gx', 'gy'), 0, 0, tiled=True)  5.05 us
    all_to_all x1, waiting for transfers between devices, body(): received = lax.all_to_all(chunk, ('gx', 'gy'), 0, 0, tiled=True)  2.05 us
    pallas_call x1, Pallas kernels, pack_edges(): pl.pallas_call(edges_kernel, out_shape=[jax.ShapeDtypeStruct((OWN_X, FIEL...  1.95 us
  transfers between devices with their start and end apart: 9, of which 6 were waited for; matrix products, arithmetic and copies ran while one was open for 1% of the time, Pallas kernels for 0%

commit v1 on v0

--- a/solution.py
+++ b/solution.py
@@ -12,10 +12,10 @@
 
 ROWS = 16
 LANES = 256
-ROW0 = 5
+ROW0 = 8
 LANE0 = 16
 EDGE = 16
-SENT = slice(4, 12)
+SENT = slice(7, 15)
 PLANES = 10
 OWN_X, OWN_Y, OWN_Z = 3, 6, 192
 FIELDS = 8
@@ -254,13 +254,14 @@
             at, held = (0, field + 3) if plane == PLANES - 1 else (plane, field)
             for half in range(2):
                 lanes = slice(128 * half, 128 * half + 128)
-                fields[field, plane, 0:1, lanes] = jnp.zeros((1, 128), jnp.float32)
+                fields[field, plane, 3:4, lanes] = jnp.zeros((1, 128), jnp.float32)
                 start = (at * 4 * 2 + half) * FIELDS + held
-                fields[field, plane, 1:5, lanes] = left[pl.ds(start, 4, stride=16), :]
+                fields[field, plane, 4:8, lanes] = left[pl.ds(start, 4, stride=16), :]
                 start = (at * 5 * 2 + half) * FIELDS + held
-                fields[field, plane, 11:16, lanes] = right[pl.ds(start, 5, stride=16), :]
+                fields[field, plane, 14:16, lanes] = right[pl.ds(start, 2, stride=16), :]
+                fields[field, plane, 0:3, lanes] = right[pl.ds(start + 32, 3, stride=16), :]
                 start = tile_row(at, 0, half) + held
-                fields[field, plane, 5:11, lanes] = planes[pl.ds(start, 6, stride=16), :]
+                fields[field, plane, 8:14, lanes] = planes[pl.ds(start, 6, stride=16), :]
     table = [
         [moduli[which : which + 1, kind : kind + 1] for kind in range(4)]
         for which in range(2)

time: 72.5 us -> 72.4 us (level)
  no operation moved by 1% of the time
where the time goes in v1:
time: 72.4 us; the launch traced here: 71.9 us
  starting transfers between devices  41 us (57%)
  waiting for transfers between devices  18.7 us (26%)
  Pallas kernels  9.54 us (13%)
  local copies, waits for them, and re-layouts  1.5 us (2%)
  between operations  0.9 us (1%)
    ppermute x8, starting transfers between devices, passed_along(): return lax.ppermute(value, axis, pairs)  35.9 us
    ppermute x8, waiting for transfers between devices, passed_along(): return lax.ppermute(value, axis, pairs)  16.6 us
    pallas_call x5, Pallas kernels, call(): pl.pallas_call(kernel, out_shape=[jax.ShapeDtypeStruct(shape, jnp.float32...  7.59 us
    all_to_all x1, starting transfers between devices, body(): received = lax.all_to_all(chunk, ('gx', 'gy'), 0, 0, tiled=True)  5.05 us
    all_to_all x1, waiting for transfers between devices, body(): received = lax.all_to_all(chunk, ('gx', 'gy'), 0, 0, tiled=True)  2.05 us
    pallas_call x1, Pallas kernels, pack_edges(): pl.pallas_call(edges_kernel, out_shape=[jax.ShapeDtypeStruct((OWN_X, FIEL...  1.95 us
  transfers between devices with their start and end apart: 9, of which 6 were waited for; matrix products, arithmetic and copies ran while one was open for 1% of the time, Pallas kernels for 0%

profile of v1, /device:TPU:1, one launch (start us, length us, event | category | flops | bytes accessed | tf_op | source)
XLA Modules:
  0.0 71.9 jit_solution(16022138722659198049)
XLA Ops:
  0.6 0.0 copy-start.1
  0.6 0.0 copy-start
  0.7 0.0 copy-start.3
  0.7 0.0 copy-start.4
  0.7 2.0 %shard_map.97 = (f32[3,8,128]{2,1,0:T(8,128)}, f32[3,8,128]{2,1,0:T(8,128)}) custom-call(f32[3,3,6,192]{3,2,1,0:T(8,128)} %guess_h.1, f32[3,3,6,192]{3,2,1,0:T(8,128)} %forcing_h.1, f32[3,6,192]{2,1,0:T(8,128)} %support_h.1, s32[3,6,192]{2,1,0:T(8,128)} %material_h.1, s32[1,2,64]{2,1,0:T(2,128)} %classes_h.1), custom_call_target="tpu_custom_call" | custom-call | tf_op jit(solution)/shard_map/pallas_call | solution.py:600
  2.6 0.0 copy-start.2
  2.6 4.8 %collective-permute-start = (f32[3,8,128]{2,1,0:T(8,128)}, f32[3,8,128]{2,1,0:T(8,128)S(1)}, u32[]{:S(2)}, u32[]{:S(2)}) collective-permute-start(f32[3,8,128]{2,1,0:T(8,128)} %get-tuple-element.18), channel_id=1, source_target_pairs={{0,1},{1,2},{2,3},{3,4},{4,5},{5,6},{6,7},{7,8},{8,9},{9,10},{10,1... | collective-permute-start | bytes 36872 | tf_op jit(solution)/shard_map/ppermute | solution.py:580
  7.5 12.2 %collective-permute-start.1 = (f32[3,8,128]{2,1,0:T(8,128)}, f32[3,8,128]{2,1,0:T(8,128)S(1)}, u32[]{:S(2)}, u32[]{:S(2)}) collective-permute-start(f32[3,8,128]{2,1,0:T(8,128)} %get-tuple-element.19), channel_id=1, source_target_pairs={{0,11},{1,0},{2,1},{3,2},{4,3},{5,4},{6,5},{7,6},{8,7},{9,8},{10,9... | collective-permute-start | bytes 36872 | tf_op jit(solution)/shard_map/ppermute | solution.py:580
  19.7 0.1 fusion.2
  19.8 0.0 copy-done.1
  19.8 0.0 copy-done
  19.8 0.0 copy-done.3
  19.8 0.0 copy-done.4
  19.9 0.0 copy-done.2
  19.9 0.1 shard_map.96
  20.0 0.0 collective-permute-done.low
  20.0 0.7 collective-permute-done.1.high
  20.7 0.1 shard_map.98
  20.8 5.9 %collective-permute-start.2 = (f32[2,6,16,128]{3,2,1,0:T(8,128)S(1)}, f32[2,6,16,128]{3,2,1,0:T(8,128)S(1)}, u32[]{:S(2)}, u32[]{:S(2)}) collective-permute-start(f32[2,6,16,128]{3,2,1,0:T(8,128)S(1)} %bitcast.20), channel_id=1, source_target_pairs={{0,576},{96,672},{192,0},{288,96},{384,192},{480,288},{576,384},{6... | collective-permute-start | bytes 294920 | tf_op jit(solution)/shard_map/ppermute | solution.py:580
  26.8 3.0 %collective-permute-start.4 = (f32[3,6,16,128]{3,2,1,0:T(8,128)S(1)}, f32[3,6,16,128]{3,2,1,0:T(8,128)S(1)}, u32[]{:S(2)}, u32[]{:S(2)}) collective-permute-start(f32[3,6,16,128]{3,2,1,0:T(8,128)S(1)} %bitcast.16), channel_id=1, source_target_pairs={{0,672},{96,0},{192,96},{288,192},{384,288},{480,384},{576,480},{6... | collective-permute-start | bytes 442376 | tf_op jit(solution)/shard_map/ppermute | solution.py:580
  29.7 2.3 %collective-permute-start.3 = (f32[2,6,16,128]{3,2,1,0:T(8,128)S(1)}, f32[2,6,16,128]{3,2,1,0:T(8,128)S(1)}, u32[]{:S(2)}, u32[]{:S(2)}) collective-permute-start(f32[2,6,16,128]{3,2,1,0:T(8,128)S(1)} %bitcast.21), channel_id=1, source_target_pairs={{0,96},{96,192},{192,288},{288,384},{384,480},{480,576},{576,672},... | collective-permute-start | bytes 294920 | tf_op jit(solution)/shard_map/ppermute | solution.py:580
  32.1 0.0 collective-permute-done.2
  32.1 0.1 or_select_fusion
  32.1 4.2 %collective-permute-done.3 = f32[2,6,16,128]{3,2,1,0:T(8,128)S(1)} collective-permute-done((f32[2,6,16,128]{3,2,1,0:T(8,128)S(1)}, f32[2,6,16,128]{3,2,1,0:T(8,128)S(1)}, u32[]{:S(2)}, u32[]{:S(2)}) %collective-permute-start.3) | collective-permute-done | bytes 98336 | tf_op jit(solution)/shard_map/ppermute | solution.py:580
  36.3 0.0 collective-permute-done.4
  36.3 0.1 fusion
  36.5 3.2 %collective-permute-start.6 = (f32[9,5,16,128]{3,2,1,0:T(8,128)S(1)}, f32[9,5,16,128]{3,2,1,0:T(8,128)S(1)}, u32[]{:S(2)}, u32[]{:S(2)}) collective-permute-start(f32[9,5,16,128]{3,2,1,0:T(8,128)S(1)} %slice.35), channel_id=1, source_target_pairs={{0,84},{12,0},{24,12},{36,24},{48,36},{60,48},{72,60},{84,72},{1,8... | collective-permute-start | bytes 1105928 | tf_op jit(solution)/shard_map/ppermute | solution.py:580
  39.8 1.1 %collective-permute-start.5 = (f32[9,4,16,128]{3,2,1,0:T(8,128)S(1)}, f32[9,4,16,128]{3,2,1,0:T(8,128)S(1)}, u32[]{:S(2)}, u32[]{:S(2)}) collective-permute-start(f32[9,4,16,128]{3,2,1,0:T(8,128)S(1)} %slice.34), channel_id=1, source_target_pairs={{0,12},{12,24},{24,36},{36,48},{48,60},{60,72},{72,84},{84,0},{1,1... | collective-permute-start | bytes 884744 | tf_op jit(solution)/shard_map/ppermute | solution.py:580
  40.9 0.0 copy-start.7
  40.9 0.7 copy-done.7
  41.6 0.0 copy-start.6
  41.6 0.1 add_bitcast_fusion.scalars
  41.6 0.6 copy-done.6
  42.2 2.3 %collective-permute-done.5 = f32[9,4,16,128]{3,2,1,0:T(8,128)S(1)} collective-permute-done((f32[9,4,16,128]{3,2,1,0:T(8,128)S(1)}, f32[9,4,16,128]{3,2,1,0:T(8,128)S(1)}, u32[]{:S(2)}, u32[]{:S(2)}) %collective-permute-start.5) | collective-permute-done | bytes 294944 | tf_op jit(solution)/shard_map/ppermute | solution.py:580
  44.6 1.8 %collective-permute-done.6 = f32[9,5,16,128]{3,2,1,0:T(8,128)S(1)} collective-permute-done((f32[9,5,16,128]{3,2,1,0:T(8,128)S(1)}, f32[9,5,16,128]{3,2,1,0:T(8,128)S(1)}, u32[]{:S(2)}, u32[]{:S(2)}) %collective-permute-start.6) | collective-permute-done | bytes 368672 | tf_op jit(solution)/shard_map/ppermute | solution.py:580
  46.3 3.8 %shard_map.99 = (f32[64,8,128]{2,1,0:T(8,128)}, f32[3,3,16,256]{3,2,1,0:T(8,128)S(1)}, f32[4,3,8,256]{3,2,1,0:T(8,128)S(1)}, f32[3,3,16,256]{3,2,1,0:T(8,128)S(1...) custom-call(f32[2,4]{1,0:T(2,128)S(1)} %broadcast_multiply_fusion.moduli, ...), custom_call_target="tpu_custom_call" | custom-call | flops 1000000 | bytes 1000000 | tf_op jit(solution)/shard_map/pallas_call | solution.py:588
  50.2 0.0 copy-start.5
  50.2 5.1 %all-to-all-start = ((f32[64,8,128]{2,1,0:T(8,128)}), f32[64,8,128]{2,1,0:T(8,128)S(1)}, u32[]{:S(2)}, u32[]{:S(2)}) async-start(f32[64,8,128]{2,1,0:T(8,128)} %get-tuple-element.26), calls=%async_computation | async-start | bytes 524288 | tf_op jit(solution)/shard_map/all_to_all | solution.py:677
  55.2 3.3 %collective-permute-start.7 = (f32[4,3,8,256]{3,2,1,0:T(8,128)S(1)}, f32[4,3,8,256]{3,2,1,0:T(8,128)S(1)}, u32[]{:S(2)}, u32[]{:S(2)}) collective-permute-start(f32[4,3,8,256]{3,2,1,0:T(8,128)S(1)} %get-tuple-element.28), channel_id=1, source_target_pairs={{0,96},{96,192},{192,288},{288,384},{384,480},{480,576},{576,672},... | collective-permute-start | bytes 294920 | tf_op jit(solution)/shard_map/ppermute | solution.py:580
  58.5 0.0 copy-done.5
  58.5 0.1 copy.13
  58.7 0.1 shard_map.95.tables
  58.8 7.6 %collective-permute-done.7.low = f32[4,3,8,256]{3,2,1,0:T(8,128)S(1)} collective-permute-done((f32[4,3,8,256]{3,2,1,0:T(8,128)S(1)}, f32[4,3,8,256]{3,2,1,0:T(8,128)S(1)}, u32[]{:S(2)}, u32[]{:S(2)}) %collective-permute-start.7) | collective-permute-done | bytes 98336 | tf_op jit(solution)/shard_map/ppermute | solution.py:580
  66.4 2.0 %all-to-all-done = f32[64,8,128]{2,1,0:T(8,128)S(1)} async-done(((f32[64,8,128]{2,1,0:T(8,128)}), f32[64,8,128]{2,1,0:T(8,128)S(1)}, u32[]{:S(2)}, u32[]{:S(2)}) %all-to-all-start) | async-done | bytes 262176 | tf_op jit(solution)/shard_map/all_to_all | solution.py:677
  68.5 3.4 %shard_map.100 = (f32[3,3,6,192]{3,2,1,0:T(8,128)}, f32[6,1,2,64]{3,2,1,0:T(2,128)}) custom-call(s32[1,5]{1,0:T(1,128)S(1)} %add_bitcast_fusion.scalars, f32[40,128]{1,0:T(8,128)S(1)} %shard_map.95.tables, f32[8,64,128]{2,1,0:T(8,128)S(1)} %bitcast.15, f32[3,3,16,256]{3,2,1,0:T(8,128)S(1)} %get-tuple-element.27.rest, ...), custom_call_target="tpu_custom_call" | custom-call | flops 1000000 | bytes 1000000 | tf_op jit(solution)/shard_map/pallas_call | solution.py:588
  (13 shorter events, 0.1 us)
Async XLA Ops:
  0.6 19.2 %copy-start.1 = (f32[3,3,6,192]{3,2,1,0:T(8,128)S(1)}, f32[3,3,6,192]{3,2,1,0:T(8,128)}, u32[]{:S(2)}) copy-start(f32[3,3,6,192]{3,2,1,0:T(8,128)} %forcing_h.1) | copy-start | bytes 124420
  0.6 19.2 %copy-start = (f32[3,3,6,192]{3,2,1,0:T(8,128)S(1)}, f32[3,3,6,192]{3,2,1,0:T(8,128)}, u32[]{:S(2)}) copy-start(f32[3,3,6,192]{3,2,1,0:T(8,128)} %guess_h.1) | copy-start | bytes 124420
  0.7 19.2 %copy-start.3 = (s32[3,6,192]{2,1,0:T(8,128)S(1)}, s32[3,6,192]{2,1,0:T(8,128)}, u32[]{:S(2)}) copy-start(s32[3,6,192]{2,1,0:T(8,128)} %material_h.1) | copy-start | bytes 41476
  0.7 19.2 %copy-start.4 = (s32[1,2,64]{2,1,0:T(2,128)S(1)}, s32[1,2,64]{2,1,0:T(2,128)}, u32[]{:S(2)}) copy-start(s32[1,2,64]{2,1,0:T(2,128)} %classes_h.1) | copy-start | bytes 1540
  2.6 17.2 %copy-start.2 = (f32[3,6,192]{2,1,0:T(8,128)S(1)}, f32[3,6,192]{2,1,0:T(8,128)}, u32[]{:S(2)}) copy-start(f32[3,6,192]{2,1,0:T(8,128)} %support_h.1) | copy-start | bytes 41476
  2.6 17.4 %collective-permute-start = (f32[3,8,128]{2,1,0:T(8,128)}, f32[3,8,128]{2,1,0:T(8,128)S(1)}, u32[]{:S(2)}, u32[]{:S(2)}) collective-permute-start(f32[3,8,128]{2,1,0:T(8,128)} %get-tuple-element.18), channel_id=1, source_target_pairs={{0,1},{1,2},{2,3},{3,4},{4,5},{5,6},{6,7},{7,8},{8,9},{9,10},{10,1... | collective-permute-start | bytes 36872 | tf_op jit(solution)/shard_map/ppermute | solution.py:580
  7.5 13.3 %collective-permute-start.1 = (f32[3,8,128]{2,1,0:T(8,128)}, f32[3,8,128]{2,1,0:T(8,128)S(1)}, u32[]{:S(2)}, u32[]{:S(2)}) collective-permute-start(f32[3,8,128]{2,1,0:T(8,128)} %get-tuple-element.19), channel_id=1, source_target_pairs={{0,11},{1,0},{2,1},{3,2},{4,3},{5,4},{6,5},{7,6},{8,7},{9,8},{10,9... | collective-permute-start | bytes 36872 | tf_op jit(solution)/shard_map/ppermute | solution.py:580
  20.8 11.2 %collective-permute-start.2 = (f32[2,6,16,128]{3,2,1,0:T(8,128)S(1)}, f32[2,6,16,128]{3,2,1,0:T(8,128)S(1)}, u32[]{:S(2)}, u32[]{:S(2)}) collective-permute-start(f32[2,6,16,128]{3,2,1,0:T(8,128)S(1)} %bitcast.20), channel_id=1, source_target_pairs={{0,576},{96,672},{192,0},{288,96},{384,192},{480,288},{576,384},{6... | collective-permute-start | bytes 294920 | tf_op jit(solution)/shard_map/ppermute | solution.py:580
  26.8 9.6 %collective-permute-start.4 = (f32[3,6,16,128]{3,2,1,0:T(8,128)S(1)}, f32[3,6,16,128]{3,2,1,0:T(8,128)S(1)}, u32[]{:S(2)}, u32[]{:S(2)}) collective-permute-start(f32[3,6,16,128]{3,2,1,0:T(8,128)S(1)} %bitcast.16), channel_id=1, source_target_pairs={{0,672},{96,0},{192,96},{288,192},{384,288},{480,384},{576,480},{6... | collective-permute-start | bytes 442376 | tf_op jit(solution)/shard_map/ppermute | solution.py:580
  29.7 6.6 %collective-permute-start.3 = (f32[2,6,16,128]{3,2,1,0:T(8,128)S(1)}, f32[2,6,16,128]{3,2,1,0:T(8,128)S(1)}, u32[]{:S(2)}, u32[]{:S(2)}) collective-permute-start(f32[2,6,16,128]{3,2,1,0:T(8,128)S(1)} %bitcast.21), channel_id=1, source_target_pairs={{0,96},{96,192},{192,288},{288,384},{384,480},{480,576},{576,672},... | collective-permute-start | bytes 294920 | tf_op jit(solution)/shard_map/ppermute | solution.py:580
  36.5 9.8 %collective-permute-start.6 = (f32[9,5,16,128]{3,2,1,0:T(8,128)S(1)}, f32[9,5,16,128]{3,2,1,0:T(8,128)S(1)}, u32[]{:S(2)}, u32[]{:S(2)}) collective-permute-start(f32[9,5,16,128]{3,2,1,0:T(8,128)S(1)} %slice.35), channel_id=1, source_target_pairs={{0,84},{12,0},{24,12},{36,24},{48,36},{60,48},{72,60},{84,72},{1,8... | collective-permute-start | bytes 1105928 | tf_op jit(solution)/shard_map/ppermute | solution.py:580
  39.8 4.8 %collective-permute-start.5 = (f32[9,4,16,128]{3,2,1,0:T(8,128)S(1)}, f32[9,4,16,128]{3,2,1,0:T(8,128)S(1)}, u32[]{:S(2)}, u32[]{:S(2)}) collective-permute-start(f32[9,4,16,128]{3,2,1,0:T(8,128)S(1)} %slice.34), channel_id=1, source_target_pairs={{0,12},{12,24},{24,36},{36,48},{48,60},{60,72},{72,84},{84,0},{1,1... | collective-permute-start | bytes 884744 | tf_op jit(solution)/shard_map/ppermute | solution.py:580
  40.9 0.7 copy-start.7
  41.6 0.7 copy-start.6
  50.2 8.4 %copy-start.5 = (f32[8,6,6]{2,0,1:T(8,128)S(1)}, f32[8,6,6]{2,0,1:T(8,128)}, u32[]{:S(2)}) copy-start(f32[8,6,6]{2,0,1:T(8,128)} %param.15) | copy-start | bytes 3460
  50.2 18.3 %all-to-all-start = ((f32[64,8,128]{2,1,0:T(8,128)}), f32[64,8,128]{2,1,0:T(8,128)S(1)}, u32[]{:S(2)}, u32[]{:S(2)}) async-start(f32[64,8,128]{2,1,0:T(8,128)} %get-tuple-element.26), calls=%async_computation | async-start | bytes 524288 | tf_op jit(solution)/shard_map/all_to_all | solution.py:677
  55.2 11.2 %collective-permute-start.7 = (f32[4,3,8,256]{3,2,1,0:T(8,128)S(1)}, f32[4,3,8,256]{3,2,1,0:T(8,128)S(1)}, u32[]{:S(2)}, u32[]{:S(2)}) collective-permute-start(f32[4,3,8,256]{3,2,1,0:T(8,128)S(1)} %get-tuple-element.28), channel_id=1, source_target_pairs={{0,96},{96,192},{192,288},{288,384},{384,480},{480,576},{576,672},... | collective-permute-start | bytes 294920 | tf_op jit(solution)/shard_map/ppermute | solution.py:580
